TPU v7x, 128 devices: a whole 4x4x4 slice. The times are simulated.
128 devices in a mesh: dp: 16 (over z, x_hi, core), tensor: 8 (over y, x_lo).
Axes of the slice: x: 4 (x_hi: 2, x_lo: 2; x = x_hi * 2 + x_lo), y: 4, z: 4, core: 2. Of those that a mesh axis runs over, the one named last changes fastest.
Arguments:
- query_states: bfloat16 [16, 512, 8192], P('dp', None, 'tensor'), may hold values from -110 to 110
- key_states: bfloat16 [16, 512, 1024], P('dp', None, 'tensor'), may hold values from -4 to 4
- value_states: bfloat16 [16, 512, 1024], P('dp', None, 'tensor'), may hold values from -6 to 6
- segment_ids: int32 [16, 512], P('dp', 'tensor'), may hold values from 0 to 7, never falling along the last dimension, each value on 1 to 256 neighbouring positions
- pair_margins: float32 [16, 4], P('dp'), may hold values from -6 to 6
- upstream: bfloat16 [16, 512, 8192], P('dp', 'tensor'), may hold values from -6 to 6
- out_weight: bfloat16 [8192, 8192], P('tensor', 'dp'), may hold values from -0.0625 to 0.0625
Outputs:
- query_grad: bfloat16 [16, 512, 8192], P('dp', None, 'tensor')
- key_grad: bfloat16 [16, 512, 1024], P('dp', None, 'tensor')
- value_grad: bfloat16 [16, 512, 1024], P('dp', None, 'tensor')
- out_weight_grad: float32 [8192, 8192], P('tensor', 'dp')
Inputs may be any that keep to these rules, and one draw needn't show every extreme that they name: `segment_ids`: every row holds all 8 responses, each of 1 to 256 positions in order.
All inputs are finite; a program needn't handle non-finite values.
Results may differ from a plain program's by a relative error of at most 0.015.
Values may be sent and summed in bfloat16 or wider, within the bound.
No kernel may reach another device: no remote copies, remote signals or barrier semaphores. Data moves between devices by JAX's collectives and lax.ppermute only.
A program may use at most 128 MiB of HBM per device.

v0:
```python
import jax
import jax.numpy as jnp
from jax import lax
from jax.sharding import PartitionSpec as P

HEADS = 64
KV_HEADS = 8
HD = 128


def shards(query_states, key_states, value_states, segment_ids, pair_margins, upstream, out_weight):
    row_count, seq_local, model_width = upstream.shape
    length = query_states.shape[1]
    head_width = query_states.shape[2]
    kv_local = key_states.shape[2] // HD
    group_size = HEADS // KV_HEADS
    score_scale = HD ** (-0.5)
    whole_segs = lax.all_gather(segment_ids, "tensor", axis=1, tiled=True)
    sigma = jax.nn.sigmoid(-pair_margins)
    onehot = (
        segment_ids[:, :, None] // 2 == jnp.arange(sigma.shape[1], dtype=jnp.int32)[None, None, :]
    ).astype(jnp.float32)
    coeff = jnp.sum(onehot * sigma[:, None, :], axis=2)
    signs = jnp.where(segment_ids % 2 == 0, -1.0, 1.0).astype(jnp.float32)
    output_grad = (upstream.astype(jnp.float32) * (signs * coeff)[:, :, None]).astype(jnp.bfloat16)
    weight_full = lax.all_gather(out_weight, "dp", axis=1, tiled=True)
    query_heads = query_states.reshape(row_count, length, kv_local, group_size, HD)
    key_heads = key_states.reshape(row_count, length, kv_local, HD)
    value_heads = value_states.reshape(row_count, length, kv_local, HD)
    position = jnp.arange(length, dtype=jnp.int32)
    allowed = (whole_segs[:, :, None] == whole_segs[:, None, :]) & (
        position[None, None, :] <= position[None, :, None]
    )
    scores = (
        jnp.einsum("rigmd,rjgd->rgmij", query_heads, key_heads, preferred_element_type=jnp.float32)
        * score_scale
    )
    scores = jnp.where(allowed[:, None, None], scores, -1e30)
    highest = jnp.max(scores, axis=-1, keepdims=True)
    expo = jnp.exp(scores - highest)
    probs = expo / jnp.sum(expo, axis=-1, keepdims=True)
    probs_low = probs.astype(jnp.bfloat16)
    attn_out = jnp.einsum(
        "rgmij,rjgd->rigmd", probs_low, value_heads, preferred_element_type=jnp.float32
    )
    attn_out = attn_out.astype(jnp.bfloat16).reshape(row_count, length, head_width)
    block_grad = lax.all_gather(output_grad, "tensor", axis=1, tiled=True)
    partial_value = jnp.einsum(
        "rte,he->rth", block_grad, weight_full, preferred_element_type=jnp.float32
    )
    wgrad_acc = jnp.einsum("rth,rte->he", attn_out, block_grad, preferred_element_type=jnp.float32)
    weight_grad = lax.psum_scatter(
        wgrad_acc.astype(jnp.bfloat16), "dp", scatter_dimension=1, tiled=True
    ).astype(jnp.float32)
    attn_grad = partial_value.astype(jnp.bfloat16)
    grad_heads = attn_grad.reshape(row_count, length, kv_local, group_size, HD)
    prob_grad = jnp.einsum(
        "rigmd,rjgd->rgmij", grad_heads, value_heads, preferred_element_type=jnp.float32
    )
    delta = jnp.sum(probs * prob_grad, axis=-1, keepdims=True)
    score_grad = (score_scale * probs * (prob_grad - delta)).astype(jnp.bfloat16)
    query_grad = jnp.einsum(
        "rgmij,rjgd->rigmd", score_grad, key_heads, preferred_element_type=jnp.float32
    )
    query_grad = query_grad.astype(jnp.bfloat16).reshape(row_count, length, head_width)
    key_grad = jnp.einsum(
        "rgmij,rigmd->rjgd", score_grad, query_heads, preferred_element_type=jnp.float32
    )
    key_grad = key_grad.astype(jnp.bfloat16).reshape(row_count, length, kv_local * HD)
    value_grad = jnp.einsum(
        "rgmij,rigmd->rjgd", probs_low, grad_heads, preferred_element_type=jnp.float32
    )
    value_grad = value_grad.astype(jnp.bfloat16).reshape(row_count, length, kv_local * HD)
    return (query_grad, key_grad, value_grad, weight_grad)


def solution(mesh):
    in_specs = (
        P("dp", None, "tensor"),
        P("dp", None, "tensor"),
        P("dp", None, "tensor"),
        P("dp", "tensor"),
        P("dp", None),
        P("dp", "tensor", None),
        P("tensor", "dp"),
    )
    out_specs = (
        P("dp", None, "tensor"),
        P("dp", None, "tensor"),
        P("dp", None, "tensor"),
        P("tensor", "dp"),
    )
    return jax.shard_map(shards, mesh=mesh, in_specs=in_specs, out_specs=out_specs, check_vma=False)
```

profile of v0, /device:TPU:1, one launch (start us, length us, event | category | flops | bytes accessed | tf_op | source)
XLA Modules:
  0.0 500.5 jit_solution(11753365866720476348)
XLA Ops:
  7.9 1.2 dynamic-slice
  11.3 2.4 multiply_convert_fusion
  14.6 1.5 copy.43
  16.1 9.9 %all-reduce = s32[512]{0:T(512)S(1)} all-reduce(s32[512]{0:T(512)S(1)} %get-tuple-element.14), channel_id=1, replica_groups=mesh['dp'=16,'tensor'=8] {'tensor'}, use_global_device_ids=true, to_apply=%add | all-reduce | flops 512 | bytes 4096 | tf_op jit(solution)/shard_map/eq | solution.py:31
  26.2 2.0 fusion.8
  28.2 3.2 copy-done.1
  31.4 1.8 fusion.7
  33.2 152.3 %all-gather.3.cloned.1.call-done = bf16[1,512,8192]{2,1,0:T(8,128)(2,1)} async-done(((bf16[1,64,8192]{2,1,0:T(8,128)(2,1)}), bf16[1,512,8192]{2,1,0:T(8,128)(2,1)}) %all-gather.3.cloned.1.call-update) | async-done | bytes 8388624 | tf_op jit(solution)/shard_map/all_gather | solution.py:47
  185.4 122.9 %all-gather.5.cloned.1.call-done = bf16[1024,8192]{1,0:T(8,128)(2,1)} async-done(((bf16[1024,512]{1,0:T(8,128)(2,1)}), bf16[1024,8192]{1,0:T(8,128)(2,1)}) %all-gather.5.cloned.1.call-update) | async-done | bytes 16777232 | tf_op jit(solution)/shard_map/all_gather | solution.py:26
  308.4 14.8 %fusion.10 = bf16[512,1024]{1,0:T(8,128)(2,1)S(1)} fusion(bf16[1024,8192]{1,0:T(8,128)(2,1)} %all-gather.5.cloned.1.call-done, bf16[1,512,8192]{2,1,0:T(8,128)(2,1)} %all-gather.3.cloned.1.call-done), kind=kOutput, calls=%fused_computation.17 | convolution fusion | flops 8590458880 | bytes 26214400 | tf_op jit(solution)/shard_map/rte,he->rth/dot_general | solution.py:48
  323.2 1.3 fusion.17
  324.5 2.1 copy-done.2
  326.6 3.4 convert_bitcast_fusion
  330.0 1.9 copy-done.4
  331.9 0.8 convolution_convert_fusion.1
  332.7 15.3 %convolution_convert_fusion = bf16[1024,8192]{1,0:T(8,128)(2,1)} fusion(bf16[512,1024]{0,1:T(8,128)(2,1)S(1)} %bitcast.143, bf16[1,512,8192]{2,1,0:T(8,128)(2,1)} %all-gather.3.cloned.1.call-done), kind=kOutput, calls=%fused_computation | convolution fusion | flops 8598323200 | bytes 26214400 | tf_op jit(solution)/shard_map/rth,rte->he/dot_general | solution.py:51
  348.0 8.2 %copy.36 = bf16[8,512,512]{2,0,1:T(8,128)(2,1)} copy(bf16[8,512,512]{1,2,0:T(8,128)(2,1)} %copy-done.4) | data formatting | bytes 8388608 | tf_op jit(solution)/shard_map/reshape.39
  356.4 10.4 %fusion.9 = bf16[8,512,512]{1,2,0:T(8,128)(2,1)S(1)} fusion(f32[512,8,512]{0,2,1:T(8,128)} %copy-done.3, f32[8,512]{1,0:T(8,128)} %get-tuple-element.13, f32[8,512]{1,0:T(8,128)} %copy-done.7, f32[8,512]{1,0:T(8,128)S(1)} %get-tuple-element.16, f32[512,512,8]{1,0,2:T(8,128)} %copy-done.1, pred[512,512]{0,1:T(8,128)(4,1)S(1)} %fusion.20), kind=kLoop, calls=%fused_computation.14 | loop fusion | flops 16777216 | bytes 21282816 | tf_op jit(solution)/shard_map/reshape.33
  366.8 2.2 copy-done.5
  369.8 1.3 copy.31
  371.2 3.8 fusion.15
  375.7 4.1 fusion.16
  379.8 111.3 %reduce-scatter.2.cloned.1.call-done = bf16[1024,512]{1,0:T(8,128)(2,1)} async-done(((bf16[1024,8192]{1,0:T(8,128)(2,1)}), bf16[1024,512]{1,0:T(8,128)(2,1)}) %reduce-scatter.2.cloned.1.call-update) | async-done | bytes 1048592 | tf_op jit(solution)/shard_map/reduce_scatter | solution.py:52
  491.2 2.8 convert_element_type.89
  (27 shorter events, 5.1 us)
Async XLA Ops:
  7.2 19.0 %copy-start = (bf16[1,512,128]{2,1,0:T(8,128)(2,1)S(1)}, bf16[1,512,128]{2,1,0:T(8,128)(2,1)}, u32[]{:S(2)}) copy-start(bf16[1,512,128]{2,1,0:T(8,128)(2,1)} %param.8) | copy-start | bytes 393220
  7.2 178.3 %all-gather.3.cloned.1.call-start = ((), (), s32[]{:S(2)}) async-start(), calls=%async_computation.1 | async-start | bytes 9437184 | tf_op jit(solution)/shard_map/all_gather | solution.py:47
  13.8 294.6 %all-gather.5.cloned.1.call-start = ((), (), s32[]{:S(2)}) async-start(), calls=%async_computation.2 | async-start | bytes 17825792 | tf_op jit(solution)/shard_map/all_gather | solution.py:26
  14.5 476.6 %reduce-scatter.2.cloned.1.call-start = ((), (), s32[]{:S(2)}) async-start(), calls=%async_computation.3 | async-start | bytes 17825792 | tf_op jit(solution)/shard_map/reduce_scatter | solution.py:52
  28.2 3.2 copy-start.1
  33.2 291.3 %copy-start.7 = (f32[8,512]{1,0:T(8,128)}, f32[8,512]{1,0:T(8,128)S(1)}, u32[]{:S(2)}) copy-start(f32[8,512]{1,0:T(8,128)S(1)} %fusion.7) | copy-start | bytes 49156
  33.2 290.1 %copy-start.6 = (bf16[1,512,128]{2,1,0:T(8,128)(2,1)S(1)}, bf16[1,512,128]{2,1,0:T(8,128)(2,1)}, u32[]{:S(2)}) copy-start(bf16[1,512,128]{2,1,0:T(8,128)(2,1)} %param.9) | copy-start | bytes 393220
  323.2 3.4 copy-start.2
  326.6 3.4 copy-start.3
  330.0 1.9 copy-start.4
  366.8 2.2 copy-start.5
Sparse Core Ops, SparseCore 0:
  13.9 171.5 all-gather.2
  187.8 120.5 all-gather.4
  348.1 143.0 reduce-scatter.1
where the time goes:
time: 501 us
  waiting for transfers between devices  387 us (77%)
  matrix products  42.8 us (9%)
  other arithmetic  23.1 us (5%)
  local copies, waits for them, and re-layouts  22.8 us (5%)
  between operations  14.6 us (3%)
  blocking collectives  9.92 us (2%)
    all_gather x1, waiting for transfers between devices, shards(): block_grad = lax.all_gather(output_grad, 'tensor', axis=1, tiled=True)  152 us
    all_gather x1, waiting for transfers between devices, shards(): weight_full = lax.all_gather(out_weight, 'dp', axis=1, tiled=True)  123 us
    reduce_scatter x1, waiting for transfers between devices, shards(): lax.psum_scatter(wgrad_acc.astype(jnp.bfloat16), 'dp', scatter_dimension=...  111 us
    dot_general x1, matrix products, shards(): jnp.einsum('rth,rte->he', attn_out, block_grad, preferred_element_type=jn...  15.3 us
    dot_general x1, matrix products, shards(): jnp.einsum('rte,he->rth', block_grad, weight_full, preferred_element_type...  14.8 us
    unnamed x22, local copies, waits for them, and re-layouts  14.6 us
    another operation x2, other arithmetic  13.7 us
  transfers between devices with their start and end apart: 3, of which 3 were waited for; matrix products, arithmetic and copies ran while one was open for 7% of the time, Pallas kernels for 0%

commit v1 on v0

--- a/solution.py
+++ b/solution.py
@@ -1,3 +1,4 @@
+import functools
 import jax
 import jax.numpy as jnp
 from jax import lax
@@ -6,6 +7,18 @@
 HEADS = 64
 KV_HEADS = 8
 HD = 128
+
+
+def define_wires_for(load, chip_axis, at_axis):
+    return jnp.concatenate(
+        jax.lax.all_to_all(
+            jnp.stack([load for _ in range(jax.lax.psum(1, chip_axis))]), chip_axis, 0, 0
+        ),
+        axis=at_axis,
+    )
+
+
+connect_the_spans = functools.partial(define_wires_for, chip_axis="dp", at_axis=1)
 
 
 def shards(query_states, key_states, value_states, segment_ids, pair_margins, upstream, out_weight):
@@ -23,7 +36,7 @@
     coeff = jnp.sum(onehot * sigma[:, None, :], axis=2)
     signs = jnp.where(segment_ids % 2 == 0, -1.0, 1.0).astype(jnp.float32)
     output_grad = (upstream.astype(jnp.float32) * (signs * coeff)[:, :, None]).astype(jnp.bfloat16)
-    weight_full = lax.all_gather(out_weight, "dp", axis=1, tiled=True)
+    weight_full = connect_the_spans(out_weight)
     query_heads = query_states.reshape(row_count, length, kv_local, group_size, HD)
     key_heads = key_states.reshape(row_count, length, kv_local, HD)
     value_heads = value_states.reshape(row_count, length, kv_local, HD)

time: 501 us -> 573 us (1.14)
  blocking collectives: 9.92 us -> 342 us
  waiting for transfers between devices: 387 us -> 115 us
  starting transfers between devices: 0.12 us -> 9.51 us
  local copies, waits for them, and re-layouts: 22.8 us -> 28.8 us
    eq x1, blocking collectives: 9.92 us -> 342 us  [shards(): whole_segs[:, :, None] == whole_segs[:, None, :]]
    all_gather x1, waiting for transfers between devices: 152 us -> 0.02 us  [shards(): block_grad = lax.all_gather(output_grad, 'tensor', axis=1, tiled=True)]
    all_gather x1 -> x0, waiting for transfers between devices: 123 us -> none  [shards(): weight_full = lax.all_gather(out_weight, 'dp', axis=1, tiled=True)]
    all_to_all x0 -> x1, starting transfers between devices: none -> 9.43 us  [define_wires_for(): jax.lax.all_to_all(jnp.stack([load for _ in range(jax.lax.psum(1, chip_ax...]
    another operation x1 -> x2, local copies, waits for them, and re-layouts: 8.18 us -> 14.1 us
    unnamed x22 -> x31, local copies, waits for them, and re-layouts: 14.6 us -> 14.7 us
  transfers between devices with their start and end apart: 3 -> 3, of which waited for: 3 -> 1; matrix products, arithmetic and copies ran while one was open for 7% -> 6% of each run, Pallas kernels for 0% -> 0%
where the time goes in v1:
time: 573 us
  blocking collectives  342 us (60%)
  waiting for transfers between devices  115 us (20%)
  matrix products  43.3 us (8%)
  local copies, waits for them, and re-layouts  28.8 us (5%)
  other arithmetic  18.9 us (3%)
  between operations  14.9 us (3%)
  starting transfers between devices  9.51 us (2%)
    eq x1, blocking collectives, shards(): whole_segs[:, :, None] == whole_segs[:, None, :]  342 us
    reduce_scatter x1, waiting for transfers between devices, shards(): lax.psum_scatter(wgrad_acc.astype(jnp.bfloat16), 'dp', scatter_dimension=...  115 us
    dot_general x1, matrix products, shards(): jnp.einsum('rth,rte->he', attn_out, block_grad, preferred_element_type=jn...  15.1 us
    dot_general x1, matrix products, shards(): jnp.einsum('rte,he->rth', block_grad, weight_full, preferred_element_type...  14.8 us
    unnamed x31, local copies, waits for them, and re-layouts  14.7 us
    another operation x2, other arithmetic  12.6 us
  transfers between devices with their start and end apart: 3, of which 1 were waited for; matrix products, arithmetic and copies ran while one was open for 6% of the time, Pallas kernels for 0%

profile of v1, /device:TPU:1, one launch (start us, length us, event | category | flops | bytes accessed | tf_op | source)
XLA Modules:
  0.0 572.6 jit_solution(12517092456815908806)
XLA Ops:
  7.2 1.5 copy.35
  8.7 6.0 %stack.2 = bf16[16,1024,512]{1,2,0:T(8,128)(2,1)} broadcast(bf16[1024,512]{0,1:T(8,128)(2,1)S(1)} %copy.35), dimensions={1,2} | broadcast | bytes 17825792 | tf_op jit(solution)/shard_map/stack | solution.py:15
  14.7 9.4 %all-to-all-start = ((bf16[16,1024,512]{1,2,0:T(8,128)(2,1)}), bf16[16,1024,512]{1,2,0:T(8,128)(2,1)}, u32[]{:S(2)}, u32[]{:S(2)}) async-start(bf16[16,1024,512]{1,2,0:T(8,128)(2,1)} %stack.2), calls=%async_computation | async-start | bytes 33554432 | tf_op jit(solution)/shard_map/all_to_all | solution.py:14
  25.7 1.2 multiply_convert_fusion
  27.3 342.0 %all-reduce = s32[512]{0:T(512)S(1)} all-reduce(s32[512]{0:T(512)S(1)} %get-tuple-element.18), channel_id=1, replica_groups=mesh['dp'=16,'tensor'=8] {'tensor'}, use_global_device_ids=true, to_apply=%add | all-reduce | flops 512 | bytes 4096 | tf_op jit(solution)/shard_map/eq | solution.py:44
  369.5 1.9 fusion.8
  371.4 3.2 copy-done.1
  374.6 1.8 fusion.7
  376.4 14.8 %fusion.10 = bf16[512,1024]{1,0:T(8,128)(2,1)S(1)} fusion(bf16[1024,8192]{0,1:T(8,128)(2,1)} %bitcast.11, bf16[1,512,8192]{2,1,0:T(8,128)(2,1)} %all-gather.2.cloned.1.call-done), kind=kOutput, calls=%fused_computation.17 | convolution fusion | flops 8590458880 | bytes 26214400 | tf_op jit(solution)/shard_map/rte,he->rth/dot_general | solution.py:61
  391.3 1.3 fusion.17
  392.5 2.1 copy-done.2
  394.7 2.7 convert_bitcast_fusion
  397.9 2.0 copy-done.4
  399.8 0.8 convolution_convert_fusion.1
  400.6 15.1 %convolution_convert_fusion = bf16[1024,8192]{1,0:T(8,128)(2,1)} fusion(bf16[512,1024]{0,1:T(8,128)(2,1)S(1)} %bitcast.146, bf16[1,512,8192]{2,1,0:T(8,128)(2,1)} %all-gather.2.cloned.1.call-done), kind=kOutput, calls=%fused_computation | convolution fusion | flops 8598323200 | bytes 26214400 | tf_op jit(solution)/shard_map/rth,rte->he/dot_general | solution.py:64
  415.8 8.1 %copy.40 = bf16[8,512,512]{2,0,1:T(8,128)(2,1)} copy(bf16[8,512,512]{1,2,0:T(8,128)(2,1)} %copy-done.4) | data formatting | bytes 8388608 | tf_op jit(solution)/shard_map/reshape.42
  423.9 9.9 %fusion.9 = bf16[8,512,512]{1,2,0:T(8,128)(2,1)S(1)} fusion(f32[512,8,512]{0,2,1:T(8,128)} %copy-done.3, f32[8,512]{1,0:T(8,128)S(1)} %get-tuple-element.17, f32[8,512]{1,0:T(8,128)S(1)} %fusion.7, f32[8,512]{1,0:T(8,128)S(1)} %get-tuple-element.20, f32[512,512,8]{1,0,2:T(8,128)} %copy-done.1, pred[512,512]{0,1:T(8,128)(4,1)S(1)} %fusion.20), kind=kLoop, calls=%fused_computation.14 | loop fusion | flops 16777216 | bytes 21282816 | tf_op jit(solution)/shard_map/reshape.36
  433.8 2.2 copy-done.5
  436.0 0.8 convolution_convert_fusion.2
  436.8 1.3 copy.43
  438.4 3.7 fusion.15
  442.9 4.9 fusion.16
  447.8 115.1 %reduce-scatter.2.cloned.1.call-done = bf16[1024,512]{1,0:T(8,128)(2,1)} async-done(((bf16[1024,8192]{1,0:T(8,128)(2,1)}), bf16[1024,512]{1,0:T(8,128)(2,1)}) %reduce-scatter.2.cloned.1.call-update) | async-done | bytes 1048592 | tf_op jit(solution)/shard_map/reduce_scatter | solution.py:65
  562.9 2.8 convert_element_type.89
  (36 shorter events, 3.0 us)
Async XLA Ops:
  7.2 362.3 %copy-start = (bf16[1,512,128]{2,1,0:T(8,128)(2,1)S(1)}, bf16[1,512,128]{2,1,0:T(8,128)(2,1)}, u32[]{:S(2)}) copy-start(bf16[1,512,128]{2,1,0:T(8,128)(2,1)} %param.8) | copy-start | bytes 393220
  14.7 9.5 %copy-start.10 = (f32[1,4]{1,0:T(1,128)S(1)}, f32[1,4]{1,0:T(1,128)}, u32[]{:S(2)}) copy-start(f32[1,4]{1,0:T(1,128)} %param.11) | copy-start | bytes 52
  14.7 9.5 %copy-start.11 = (u32[128]{0:T(128)S(1)}, u32[128]{0:T(128)}, u32[]{:S(2)}) copy-start(u32[128]{0:T(128)} %constant.49) | copy-start | bytes 1540
  14.7 10.8 %copy-start.9 = (s32[1,64]{1,0:T(1,128)S(1)}, s32[1,64]{1,0:T(1,128)}, u32[]{:S(2)}) copy-start(s32[1,64]{1,0:T(1,128)} %param.10) | copy-start | bytes 772
  14.7 11.0 %copy-start.6 = (bf16[1,64,8192]{2,1,0:T(8,128)(2,1)S(1)}, bf16[1,64,8192]{2,1,0:T(8,128)(2,1)}, u32[]{:S(2)}) copy-start(bf16[1,64,8192]{2,1,0:T(8,128)(2,1)} %param.12) | copy-start | bytes 3145732
  14.7 12.3 %copy-start.7 = (bf16[1,512,1024]{2,1,0:T(8,128)(2,1)S(1)}, bf16[1,512,1024]{2,1,0:T(8,128)(2,1)}, u32[]{:S(2)}) copy-start(bf16[1,512,1024]{2,1,0:T(8,128)(2,1)} %param.7) | copy-start | bytes 3145732
  14.7 361.7 %all-to-all-start = ((bf16[16,1024,512]{1,2,0:T(8,128)(2,1)}), bf16[16,1024,512]{1,2,0:T(8,128)(2,1)}, u32[]{:S(2)}, u32[]{:S(2)}) async-start(bf16[16,1024,512]{1,2,0:T(8,128)(2,1)} %stack.2), calls=%async_computation | async-start | bytes 33554432 | tf_op jit(solution)/shard_map/all_to_all | solution.py:14
  24.1 352.3 %all-gather.2.cloned.1.call-start = ((), (), s32[]{:S(2)}) async-start(), calls=%async_computation.2 | async-start | bytes 9437184 | tf_op jit(solution)/shard_map/all_gather | solution.py:60
  26.9 536.0 %reduce-scatter.2.cloned.1.call-start = ((), (), s32[]{:S(2)}) async-start(), calls=%async_computation.3 | async-start | bytes 17825792 | tf_op jit(solution)/shard_map/reduce_scatter | solution.py:65
  371.4 3.2 copy-start.1
  376.4 14.8 %copy-start.8 = (bf16[1,512,128]{2,1,0:T(8,128)(2,1)S(1)}, bf16[1,512,128]{2,1,0:T(8,128)(2,1)}, u32[]{:S(2)}) copy-start(bf16[1,512,128]{2,1,0:T(8,128)(2,1)} %param.9) | copy-start | bytes 393220
  391.3 3.4 copy-start.2
  394.7 3.2 copy-start.3
  397.9 2.0 copy-start.4
  433.8 2.2 copy-start.5
Sparse Core Ops, SparseCore 0:
  27.2 327.0 all-gather.1
  415.9 146.9 reduce-scatter.1
